TPU v7x, 32 devices: a whole 2x2x4 slice. The times are simulated.
32 devices in a mesh: groups: 1, stat: 32 (over z, y, x, core).
Axes of the slice: x: 2, y: 2, z: 4, core: 2. Of those that a mesh axis runs over, the one named last changes fastest.
Arguments:
- predicted_moments: bfloat16 [256, 65536], P(('groups', 'stat')), may hold values from -24 to 24
- member_vectors: bfloat16 [256, 32768], P(('groups', 'stat')), may hold values from -6 to 6
- measured_moments: float32 [65536], P(('groups', 'stat')), may hold values from -96 to 96
- block_error_group: int32 [128], P(('groups', 'stat')), may hold values from 0 to 23
- group_error_spread: float32 [24], P('groups'), may hold values from 0.08 to 64
- background_spread: float32 [1], P('groups'), may hold values from 11.313708 to 45.254833
- member_random_keys: int32 [256], P('groups'), may hold values from 0 to 16777215
Outputs:
- updated: bfloat16 [256, 32768], P(('groups', 'stat'))
- predicted: bfloat16 [256, 65536], P('groups', 'stat')
All inputs are finite; a program needn't handle non-finite values.
Results may differ from a plain program's by a relative error of at most 0.008.
The roundings to bfloat16 on the way count: a program that leaves them out, or rounds other values in their place, can miss the bound.
Values may be sent and summed in bfloat16 or wider, within the bound.
A program may use at most 64 MiB of HBM per device.

v0:
```python
import math

import jax
import jax.numpy as jnp
from jax import lax
from jax.sharding import PartitionSpec as P

SLAB = 512


seed_factor = 668265261
index_factor = 374761393
scramble_one = 2146121005
scramble_two = 739982445


def scramble(hashed):
    hashed = hashed ^ lax.shift_right_logical(hashed, jnp.int32(16))
    hashed = hashed * scramble_one
    hashed = hashed ^ lax.shift_right_logical(hashed, jnp.int32(15))
    hashed = hashed * scramble_two
    return hashed ^ lax.shift_right_logical(hashed, jnp.int32(16))


def uniform_from(hashed):
    quotient = lax.shift_right_logical(scramble(hashed), jnp.int32(9))
    return (quotient.astype(jnp.float32) + 0.5) * 2.0 ** (-23)


def normal_draw(member_random_keys, position):
    hashed = member_random_keys[:, None] * seed_factor + position[None, :] * index_factor
    first_part = uniform_from(hashed)
    second_part = uniform_from(hashed + 1)
    return jnp.sqrt(-2.0 * jnp.log(first_part)) * jnp.cos(2.0 * math.pi * second_part)


def inner(left, right):
    return lax.dot_general(
        left, right, (((1,), (1,)), ((), ())), preferred_element_type=jnp.float32
    )


def transposed_product(weights, right):
    return lax.dot_general(
        weights, right, (((0,), (0,)), ((), ())), preferred_element_type=jnp.float32
    )


def solve_system(gram, right):
    system = jnp.eye(gram.shape[0], dtype=jnp.float32) + gram
    factor = jnp.linalg.cholesky(system)
    middle = lax.linalg.triangular_solve(factor, right, left_side=True, lower=True)
    return lax.linalg.triangular_solve(factor, middle, left_side=True, lower=True, transpose_a=True)


def body(
    predicted_moments,
    member_vectors,
    measured_moments,
    block_error_group,
    group_error_spread,
    background_spread,
    member_random_keys,
):
    devices_total = lax.axis_size("stat")
    device_rank = lax.axis_index("stat")
    stat_width = measured_moments.shape[0]
    par_width = member_vectors.shape[1] // devices_total
    members = member_random_keys.shape[0]
    root_scale = math.sqrt(members - 1.0)
    prior = background_spread[0]
    shard_result_lines = lax.all_to_all(
        predicted_moments, "stat", split_axis=1, concat_axis=0, tiled=True
    )
    params_rows = lax.all_to_all(member_vectors, "stat", split_axis=1, concat_axis=0, tiled=True)
    classes = group_error_spread.shape[0]
    selector = (block_error_group[:, None] == jnp.arange(classes, dtype=jnp.int32)[None, :]).astype(
        jnp.float32
    )
    slab_sigma = jnp.dot(selector, group_error_spread, precision=lax.Precision.HIGHEST)
    sigma = jnp.broadcast_to(slab_sigma[:, None], (block_error_group.shape[0], SLAB)).reshape(
        stat_width
    )
    closure_results = shard_result_lines.astype(jnp.float32)
    out_average = jnp.mean(closure_results, axis=0)
    anomaly = ((closure_results - out_average) / (sigma * root_scale)).astype(jnp.bfloat16)
    stat_position = device_rank * stat_width + jnp.arange(stat_width, dtype=jnp.int32)
    misfit = (
        (measured_moments - closure_results) / sigma
        + normal_draw(member_random_keys, stat_position)
    ).astype(jnp.bfloat16)
    params = params_rows.astype(jnp.float32)
    par_average = jnp.mean(params, axis=0)
    spread = ((params - par_average) / root_scale).astype(jnp.bfloat16)
    par_position = (
        devices_total * stat_width
        + device_rank * par_width
        + jnp.arange(par_width, dtype=jnp.int32)
    )
    prior_misfit = (-params / prior + normal_draw(member_random_keys, par_position)).astype(
        jnp.bfloat16
    )
    gram_part = inner(anomaly, anomaly) + inner(spread, spread) / (prior * prior)
    cross_part = inner(anomaly, misfit) + inner(spread, prior_misfit) / prior
    gram, cross = lax.psum((gram_part, cross_part), "stat")
    weights = solve_system(gram, cross).astype(jnp.bfloat16)
    updated_rows = (params + transposed_product(weights, spread)).astype(jnp.bfloat16)
    updated = lax.all_to_all(updated_rows, "stat", split_axis=0, concat_axis=1, tiled=True)
    predicted = (closure_results + sigma[None, :] * transposed_product(weights, anomaly)).astype(
        jnp.bfloat16
    )
    return (updated, predicted)


def solution(mesh):
    placed = (
        P(("groups", "stat"), None),
        P(("groups", "stat"), None),
        P(("groups", "stat")),
        P(("groups", "stat")),
        P("groups"),
        P("groups"),
        P("groups"),
    )
    return jax.shard_map(
        body,
        mesh=mesh,
        in_specs=placed,
        out_specs=(P(("groups", "stat"), None), P("groups", "stat")),
        check_vma=False,
    )
```

profile of v0, /device:TPU:0, one launch (start us, length us, event | category | flops | bytes accessed | tf_op | source)
XLA Modules:
  0.0 295.2 jit_solution(2105899509149193762)
XLA Ops:
  7.2 0.0 copy-start
  7.2 22.9 %all_to_all.45 = bf16[8,32,1024]{2,0,1:T(8,128)(2,1)S(1)} all-to-all(bf16[8,32,1024]{2,0,1:T(8,128)(2,1)} %bitcast.126), channel_id=1, replica_groups=mesh['groups'=1,'stat'=32] {'stat'}, dimensions={1} | all-to-all | bytes 1048576 | tf_op jit(solution)/shard_map/all_to_all | solution.py:75
  30.0 3.1 %all-to-all-start.1 = ((bf16[8,32,2048]{2,0,1:T(8,128)(2,1)}), bf16[8,32,2048]{2,0,1:T(8,128)(2,1)S(1)}, u32[]{:S(2)}, u32[]{:S(2)}) async-start(bf16[8,32,2048]{2,0,1:T(8,128)(2,1)} %bitcast.3), calls=%async_computation.1 | async-start | bytes 2097152 | tf_op jit(solution)/shard_map/all_to_all | solution.py:72
  33.1 0.0 all-reduce.4.cloned.1.call-start
  33.2 0.0 copy-done
  33.2 0.0 copy-done.5
  33.2 0.2 convolution_bitcast_fusion
  33.4 0.1 broadcast_bitcast_fusion
  33.5 0.0 copy-done.3
  33.5 0.1 add.134
  34.3 0.1 convert_reduce_fusion.1
  34.4 25.0 %all-to-all-done.1 = bf16[8,32,2048]{2,0,1:T(8,128)(2,1)S(1)} async-done(((bf16[8,32,2048]{2,0,1:T(8,128)(2,1)}), bf16[8,32,2048]{2,0,1:T(8,128)(2,1)S(1)}, u32[]{:S(2)}, u32[]{:S(2)}) %all-to-all-start.1) | async-done | bytes 1048608 | tf_op jit(solution)/shard_map/all_to_all | solution.py:72
  59.4 0.2 convert_reduce_fusion
  59.5 0.0 copy-start.4
  59.6 0.6 fusion.130
  60.2 0.0 copy-done.4
  60.2 9.9 %fusion.63 = f32[256,256]{1,0:T(8,128)S(1)} fusion(bf16[8,32,2048]{2,0,1:T(8,128)(2,1)S(1)} %all-to-all-done.1, s32[2048]{0:T(1024)S(1)} %add_multiply_fusion, s32[32,8]{1,0:T(8,128)S(1)} %add.134, f32[2048]{0:T(1024)S(1)} %bitcast.128, f32[2048]{0:T(1024)S(1)} %copy-done.4, f32[2048]{0:T(1024)S(1)} %broadcast_multiply_fusion, ...), kind=kOutput, calls=%fused_computation.97 | convolution fusion | flops 287834112 | bytes 1352704 | tf_op jit(solution)/shard_map/dot_general | solution.py:38
  70.2 1.1 fusion.32
  71.2 5.9 %fusion.33 = f32[256,256]{1,0:T(8,128)} fusion(f32[256,256]{1,0:T(8,128)S(1)} %fusion.63, bf16[8,32,1024]{2,0,1:T(8,128)(2,1)S(1)} %all_to_all.45, s32[1024]{0:T(1024)S(1)} %add_multiply_fusion.1, s32[32,8]{1,0:T(8,128)S(1)} %add.134, f32[]{:T(128)} %bitcast.124, f32[1024]{0:T(1024)S(1)} %broadcast_multiply_fusion.2), kind=kOutput, calls=%fused_computation.62 | convolution fusion | flops 144048128 | bytes 1057796 | tf_op jit(solution)/shard_map/dot_general | solution.py:38
  77.2 0.0 all-reduce.4.cloned.1.call-update
  77.2 127.3 %all-reduce.4.cloned.1.call-done = (f32[256,256]{1,0:T(8,128)}, f32[256,256]{0,1:T(8,128)}) async-done(((f32[256,256]{1,0:T(8,128)}, f32[256,256]{0,1:T(8,128)}), (f32[256,256]{1,0:T(8,128)}, f32[256,256]{0,1:T(8,128)})) %all-reduce.4.cloned.1.call-update) | async-done | bytes 524304 | tf_op jit(solution)/shard_map/psum | solution.py:105
  204.5 1.0 convert_add_fusion
  205.6 0.1 copy.14
  205.7 0.0 copy-done.1
  205.8 11.7 %cholesky.50 = f32[128,128]{1,0:T(8,128)S(1)} custom-call(f32[128,128]{1,0:T(8,128)S(1)} %cholesky.118), custom_call_target="Cholesky" | custom-call | tf_op jit(solution)/shard_map/jit(cholesky)/cholesky | solution.py:51
  217.6 9.8 %custom-call.16 = f32[1,128,128]{1,2,0:T(8,128)S(1)} custom-call(f32[1,128,128]{2,1,0:T(8,128)S(1)} %get-tuple-element.25), custom_call_target="InvertDiagBlocksLowerTriangular" | custom-call | tf_op jit(solution)/shard_map/jit(cholesky)/cholesky | solution.py:51
  227.4 0.2 constant_dynamic-update-slice_fusion.1
  227.6 0.3 convolution_subtract_fusion.2
  227.9 11.9 %cholesky.105 = f32[128,128]{1,0:T(8,128)S(1)} custom-call(f32[128,128]{1,0:T(8,128)S(1)} %convolution_subtract_fusion.2), custom_call_target="Cholesky" | custom-call | tf_op jit(solution)/shard_map/jit(cholesky)/cholesky | solution.py:51
  239.8 0.6 compare_reduce_fusion
  241.8 0.1 triangular_solve.69
  241.9 4.0 %while.1 = (s32[]{:T(128)}, f32[256,256]{1,0:T(8,128)S(1)}, s32[2,2]{1,0:T(2,128)S(1)}, f32[2,128,128]{2,1,0:T(8,128)S(1)}, s32[]{:T(128)}) while((s32[]{:T(128)}, f32[256,256]{1,0:T(8,128)S(1)}, s32[2,2]{1,0:T(2,128)S(1)}, f32[2,128,128]{2,1,0:T(8,128)S(1)}, s32[]{:T(128)}) %tuple.28), condition=%wide.while_cond, body=%wide.while_body.sunk | while | flops 2 | bytes 131181 | solution.py:53
  241.9 0.6 fusion.140
  242.5 1.4 bitcast_dynamic-update-slice_fusion.2
  243.9 0.6 fusion.140
  244.5 1.4 bitcast_dynamic-update-slice_fusion.2
  245.9 19.7 %custom-call.17 = f32[2,128,128]{1,2,0:T(8,128)S(1)} custom-call(f32[2,128,128]{2,1,0:T(8,128)S(1)} %get-tuple-element.9), custom_call_target="InvertDiagBlocksLowerTriangular" | custom-call | tf_op jit(solution)/shard_map/triangular_solve | solution.py:53
  265.6 0.3 fusion.91
  265.9 0.3 convolution_subtract_fusion.1
  266.1 0.3 fusion.97
  266.5 0.3 fusion.128
  266.7 0.3 convolution_subtract_fusion
  267.0 0.3 convolution_convert_fusion
  267.3 1.1 fusion.31
  268.4 3.6 %all-to-all-start.2 = ((bf16[32,8,1024]{2,1,0:T(8,128)(2,1)}), bf16[32,8,1024]{2,1,0:T(8,128)(2,1)S(1)}, u32[]{:S(2)}, u32[]{:S(2)}) async-start(bf16[32,8,1024]{2,1,0:T(8,128)(2,1)} %fusion.31), calls=%async_computation.2 | async-start | bytes 1048576 | tf_op jit(solution)/shard_map/all_to_all | solution.py:108
  272.1 1.6 fusion.2
  273.6 14.0 %all-to-all-done.2 = bf16[32,8,1024]{2,1,0:T(8,128)(2,1)S(1)} async-done(((bf16[32,8,1024]{2,1,0:T(8,128)(2,1)}), bf16[32,8,1024]{2,1,0:T(8,128)(2,1)S(1)}, u32[]{:S(2)}, u32[]{:S(2)}) %all-to-all-start.2) | async-done | bytes 524320 | tf_op jit(solution)/shard_map/all_to_all | solution.py:108
  287.6 0.8 copy.33
  (22 shorter events, 0.2 us)
Async XLA Ops:
  7.2 26.0 %copy-start = (f32[24]{0:T(128)S(1)}, f32[24]{0:T(128)}, u32[]{:S(2)}) copy-start(f32[24]{0:T(128)} %param.11) | copy-start | bytes 292
  30.0 3.2 %copy-start.5 = (s32[4]{0:T(128)S(1)}, s32[4]{0:T(128)}, u32[]{:S(2)}) copy-start(s32[4]{0:T(128)} %param.10) | copy-start | bytes 52
  30.0 3.4 %copy-start.3 = (s32[256]{0:T(256)S(1)}, s32[256]{0:T(256)}, u32[]{:S(2)}) copy-start(s32[256]{0:T(256)} %param.13) | copy-start | bytes 3076
  30.0 29.3 %all-to-all-start.1 = ((bf16[8,32,2048]{2,0,1:T(8,128)(2,1)}), bf16[8,32,2048]{2,0,1:T(8,128)(2,1)S(1)}, u32[]{:S(2)}, u32[]{:S(2)}) async-start(bf16[8,32,2048]{2,0,1:T(8,128)(2,1)} %bitcast.3), calls=%async_computation.1 | async-start | bytes 2097152 | tf_op jit(solution)/shard_map/all_to_all | solution.py:72
  33.1 171.4 %all-reduce.4.cloned.1.call-start = ((), (), s32[]{:S(2)}) async-start(), calls=%async_computation.3 | async-start | bytes 1048576 | tf_op jit(solution)/shard_map/psum | solution.py:105
  59.5 0.7 copy-start.4
  204.5 1.2 copy-start.1
  217.6 48.0 %copy-start.2 = (f32[256,256]{1,0:T(8,128)S(1)}, f32[256,256]{1,0:T(8,128)}, u32[]{:S(2)}) copy-start(f32[256,256]{1,0:T(8,128)} %get-tuple-element.18) | copy-start | bytes 786436
  268.4 19.2 %all-to-all-start.2 = ((bf16[32,8,1024]{2,1,0:T(8,128)(2,1)}), bf16[32,8,1024]{2,1,0:T(8,128)(2,1)S(1)}, u32[]{:S(2)}, u32[]{:S(2)}) async-start(bf16[32,8,1024]{2,1,0:T(8,128)(2,1)} %fusion.31), calls=%async_computation.2 | async-start | bytes 1048576 | tf_op jit(solution)/shard_map/all_to_all | solution.py:108
Sparse Core Ops, SparseCore 0:
  77.3 127.1 all-reduce.3
where the time goes:
time: 296 us; the launch traced here: 295 us
  waiting for transfers between devices  166 us (56%)
  other arithmetic  55.2 us (19%)
  blocking collectives  22.9 us (8%)
  matrix products  22.6 us (8%)
  between operations  16.3 us (6%)
  starting transfers between devices  6.71 us (2%)
  local copies, waits for them, and re-layouts  5.2 us (2%)
    psum x1, waiting for transfers between devices, body(): gram, cross = lax.psum((gram_part, cross_part), 'stat')  127 us
    another operation x6, other arithmetic, solve_system(): factor = jnp.linalg.cholesky(system)  34.2 us
    all_to_all x1, waiting for transfers between devices, body(): lax.all_to_all(predicted_moments, 'stat', split_axis=1, concat_axis=0, ti...  25 us
    all_to_all x1, blocking collectives, body(): lax.all_to_all(member_vectors, 'stat', split_axis=1, concat_axis=0, tiled...  22.9 us
    another operation x3, other arithmetic, solve_system(): lax.linalg.triangular_solve(factor, middle, left_side=True, lower=True, t...  19.7 us
    dot_general x4, matrix products, inner(): lax.dot_general(left, right, (((1,), (1,)), ((), ())), preferred_element_...  17.6 us
    all_to_all x1, waiting for transfers between devices, body(): lax.all_to_all(updated_rows, 'stat', split_axis=0, concat_axis=1, tiled=T...  14 us
  transfers between devices with their start and end apart: 3, of which 3 were waited for; matrix products, arithmetic and copies ran while one was open for 1% of the time, Pallas kernels for 0%

commit v1 on v0

--- a/solution.py
+++ b/solution.py
@@ -1,12 +1,17 @@
+import functools
 import math
 
 import jax
 import jax.numpy as jnp
 from jax import lax
+from jax.experimental import pallas as pl
+from jax.experimental.pallas import tpu as pltpu
 from jax.sharding import PartitionSpec as P
 
 SLAB = 512
-
+LANES = 128
+BLOCK = 16
+MESH = pl.DeviceIdType.MESH
 
 seed_factor = 668265261
 index_factor = 374761393
@@ -46,11 +51,201 @@
     )
 
 
-def solve_system(gram, right):
-    system = jnp.eye(gram.shape[0], dtype=jnp.float32) + gram
-    factor = jnp.linalg.cholesky(system)
-    middle = lax.linalg.triangular_solve(factor, right, left_side=True, lower=True)
-    return lax.linalg.triangular_solve(factor, middle, left_side=True, lower=True, transpose_a=True)
+def stages_of(mesh_size):
+    rest = mesh_size // 2
+    second = 1
+    while second * second < rest:
+        second *= 2
+    return ((1, 2), (2, second), (2 * second, rest // second))
+
+
+def sum_kernel(stages, x_ref, o_ref, *scratch):
+    count = len(stages)
+    recvs = scratch[:count]
+    totals = scratch[count : 2 * count]
+    gathered, send_sem, recv_sem, gsend_sem, grecv_sem = scratch[2 * count :]
+    me = lax.axis_index("stat")
+    digits = [lax.rem(lax.div(me, stride), size) for stride, size in stages]
+
+    def peer(t, offset):
+        stride, size = stages[t]
+        other = lax.rem(digits[t] + offset, size)
+        return other, me + (other - digits[t]) * stride
+
+    barrier = pltpu.get_barrier_semaphore()
+    peers = 0
+    for t, (stride, size) in enumerate(stages):
+        for offset in range(1, size):
+            pl.semaphore_signal(
+                barrier, inc=1, device_id={"stat": peer(t, offset)[1]}, device_id_type=MESH
+            )
+            peers += 1
+    pl.semaphore_wait(barrier, peers)
+
+    source = x_ref
+    length = x_ref.shape[0]
+    bases = [0]
+    slot = 0
+    for t, (stride, size) in enumerate(stages):
+        piece = length // size
+        copies = []
+        for offset in range(1, size):
+            other, device = peer(t, offset)
+            copy = pltpu.make_async_remote_copy(
+                src_ref=source.at[pl.ds(other * piece, piece)],
+                dst_ref=recvs[t].at[offset - 1],
+                send_sem=send_sem.at[slot],
+                recv_sem=recv_sem.at[slot],
+                device_id={"stat": device},
+                device_id_type=MESH,
+            )
+            copy.start()
+            copies.append(copy)
+            slot += 1
+        value = source[pl.ds(digits[t] * piece, piece)]
+        for offset in range(1, size):
+            copies[offset - 1].wait_recv()
+            value = value + recvs[t][offset - 1]
+        totals[t][...] = value
+        for copy in copies:
+            copy.wait_send()
+        bases.append(bases[t] + digits[t] * piece)
+        source, length = totals[t], piece
+
+    gathered[pl.ds(bases[count], length)] = source[...]
+    slot = 0
+    for t in reversed(range(count)):
+        stride, size = stages[t]
+        copies = []
+        for offset in range(1, size):
+            _, device = peer(t, offset)
+            own = gathered.at[pl.ds(bases[t + 1], length)]
+            copy = pltpu.make_async_remote_copy(
+                src_ref=own,
+                dst_ref=own,
+                send_sem=gsend_sem.at[slot],
+                recv_sem=grecv_sem.at[slot],
+                device_id={"stat": device},
+                device_id_type=MESH,
+            )
+            copy.start()
+            copies.append(copy)
+            slot += 1
+        for copy in copies:
+            copy.wait()
+        length *= size
+    o_ref[...] = gathered[...]
+
+
+def sum_over_devices(part, devices_total):
+    rows, columns = part.shape
+    chunks = max(rows // 8, devices_total)
+    spread = chunks // (rows // 8)
+    width = columns // spread
+    packed = part.reshape(rows // 8, 8, spread, width).transpose(0, 2, 1, 3)
+    packed = packed.reshape(chunks, 8, width)
+    stages = stages_of(devices_total)
+    recvs, totals, length, copies = [], [], chunks, 0
+    for stride, size in stages:
+        length //= size
+        recvs.append(pltpu.VMEM((size - 1, length, 8, width), jnp.float32))
+        totals.append(pltpu.VMEM((length, 8, width), jnp.float32))
+        copies += size - 1
+    whole = pl.BlockSpec(memory_space=pltpu.VMEM)
+    out = pl.pallas_call(
+        functools.partial(sum_kernel, stages),
+        out_shape=jax.ShapeDtypeStruct(packed.shape, jnp.float32),
+        in_specs=[whole],
+        out_specs=whole,
+        scratch_shapes=recvs
+        + totals
+        + [pltpu.VMEM(packed.shape, jnp.float32)]
+        + [pltpu.SemaphoreType.DMA((copies,))] * 4,
+        compiler_params=pltpu.CompilerParams(
+            collective_id=0, has_side_effects=True, vmem_limit_bytes=16 * 2**20
+        ),
+        name="sum_over_devices",
+    )(packed)
+    return out.reshape(rows // 8, spread, 8, width).transpose(0, 2, 1, 3).reshape(rows, columns)
+
+
+def exact_dot(left, right):
+    return jnp.dot(
+        left, right, preferred_element_type=jnp.float32, precision=lax.Precision.HIGHEST
+    )
+
+
+def solve_kernel(s_ref, w_ref, m_ref):
+    size = s_ref.shape[0]
+    groups = s_ref.shape[1] // LANES
+    own = size // LANES
+    row = lax.broadcasted_iota(jnp.int32, (size, size), 0)
+    column = lax.broadcasted_iota(jnp.int32, (size, size), 1)
+    m_ref[:, :size] = s_ref[:, :size] + (row == column).astype(jnp.float32)
+    m_ref[:, size:] = s_ref[:, size:]
+    row_id = lax.broadcasted_iota(jnp.int32, (BLOCK, LANES), 0)
+    for start in range(0, size, BLOCK):
+        group = start // LANES
+        lane = start % LANES
+        panel = [
+            m_ref[start : start + BLOCK, g * LANES : (g + 1) * LANES]
+            for g in range(group, groups)
+        ]
+        head = panel[0]
+        splat = [
+            jnp.broadcast_to(head[:, lane + j : lane + j + 1], (BLOCK, LANES))
+            for j in range(BLOCK)
+        ]
+        for j in range(BLOCK):
+            inverse = 1.0 / splat[j][j : j + 1, :]
+            at_pivot = row_id == j
+            factor = splat[j]
+
+            def step(block):
+                scaled = block[j : j + 1, :] * inverse
+                return jnp.where(at_pivot, scaled, block - factor * scaled)
+
+            for later in range(j + 1, BLOCK):
+                splat[later] = step(splat[later])
+            panel = [step(block) for block in panel]
+        top = jnp.concatenate(panel, axis=1)
+        pieces = []
+        if lane > 0:
+            pieces.append(jnp.zeros((lane, top.shape[1]), jnp.float32))
+        pieces.append(top)
+        if lane + BLOCK < LANES:
+            pieces.append(jnp.zeros((LANES - lane - BLOCK, top.shape[1]), jnp.float32))
+        right = jnp.concatenate(pieces, axis=0)
+        left = m_ref[:, group * LANES : (group + 1) * LANES]
+        from_column = group * LANES
+        after = start + BLOCK
+        spans = []
+        if after < size:
+            spans.append((after, after + BLOCK))
+            if after + BLOCK < size:
+                spans.append((after + BLOCK, size))
+        if start > 0:
+            spans.append((0, start))
+        for low, high in spans:
+            m_ref[low:high, from_column:] = m_ref[low:high, from_column:] - exact_dot(
+                left[low:high], right
+            )
+        m_ref[start:after, from_column:] = top
+    w_ref[...] = m_ref[:, size:].astype(w_ref.dtype)
+
+
+def solve_system(total):
+    size = total.shape[0]
+    whole = pl.BlockSpec(memory_space=pltpu.VMEM)
+    return pl.pallas_call(
+        solve_kernel,
+        out_shape=jax.ShapeDtypeStruct((size, total.shape[1] - size), jnp.bfloat16),
+        in_specs=[whole],
+        out_specs=whole,
+        scratch_shapes=[pltpu.VMEM(total.shape, jnp.float32)],
+        compiler_params=pltpu.CompilerParams(vmem_limit_bytes=16 * 2**20),
+        name="solve_system",
+    )(total)
 
 
 def body(
@@ -102,8 +297,8 @@
     )
     gram_part = inner(anomaly, anomaly) + inner(spread, spread) / (prior * prior)
     cross_part = inner(anomaly, misfit) + inner(spread, prior_misfit) / prior
-    gram, cross = lax.psum((gram_part, cross_part), "stat")
-    weights = solve_system(gram, cross).astype(jnp.bfloat16)
+    total = sum_over_devices(jnp.concatenate([gram_part, cross_part], axis=1), devices_total)
+    weights = solve_system(total)
     updated_rows = (params + transposed_product(weights, spread)).astype(jnp.bfloat16)
     updated = lax.all_to_all(updated_rows, "stat", split_axis=0, concat_axis=1, tiled=True)
     predicted = (closure_results + sigma[None, :] * transposed_product(weights, anomaly)).astype(

time: 296 us -> 120 us (0.41)
  waiting for transfers between devices: 166 us -> 39 us
  other arithmetic: 55.2 us -> 0.38 us
  Pallas kernels: 0 us -> 29.6 us
  between operations: 16.3 us -> 1.44 us
  local copies, waits for them, and re-layouts: 5.2 us -> 1.22 us
  matrix products: 22.6 us -> 18.9 us
    psum x1 -> x0, waiting for transfers between devices: 127 us -> none  [body(): gram, cross = lax.psum((gram_part, cross_part), 'stat')]
    another operation x9 -> x0, other arithmetic: 53.9 us -> none  [the longest x6 34.2 us: solve_system(): factor = jnp.linalg.cholesky(system)]
    pallas_call x0 -> x2, Pallas kernels: none -> 29.6 us  [the longest x1 21.9 us: sum_over_devices(): pl.pallas_call(functools.partial(sum_kernel, stages), out_shape=jax.Shape...]
    another operation x9 -> x0, local copies, waits for them, and re-layouts: 4.05 us -> none
  transfers between devices with their start and end apart: 3 -> 2, of which waited for: 3 -> 2; matrix products, arithmetic and copies ran while one was open for 1% -> 2% of each run, Pallas kernels for 0% -> 0%
where the time goes in v1:
time: 120 us
  waiting for transfers between devices  39 us (32%)
  Pallas kernels  29.6 us (25%)
  blocking collectives  22.9 us (19%)
  matrix products  18.9 us (16%)
  starting transfers between devices  6.6 us (6%)
  between operations  1.44 us (1%)
  local copies, waits for them, and re-layouts  1.22 us (1%)
    all_to_all x1, waiting for transfers between devices, body(): lax.all_to_all(predicted_moments, 'stat', split_axis=1, concat_axis=0, ti...  25 us
    all_to_all x1, blocking collectives, body(): lax.all_to_all(member_vectors, 'stat', split_axis=1, concat_axis=0, tiled...  22.9 us
    pallas_call x1, Pallas kernels, sum_over_devices(): pl.pallas_call(functools.partial(sum_kernel, stages), out_shape=jax.Shape...  21.9 us
    dot_general x4, matrix products, inner(): lax.dot_general(left, right, (((1,), (1,)), ((), ())), preferred_element_...  16 us
    all_to_all x1, waiting for transfers between devices, body(): lax.all_to_all(updated_rows, 'stat', split_axis=0, concat_axis=1, tiled=T...  14 us
    pallas_call x1, Pallas kernels, solve_system(): pl.pallas_call(solve_kernel, out_shape=jax.ShapeDtypeStruct((size, total....  7.72 us
    all_to_all x1, starting transfers between devices, body(): lax.all_to_all(updated_rows, 'stat', split_axis=0, concat_axis=1, tiled=T...  3.53 us
    all_to_all x1, starting transfers between devices, body(): lax.all_to_all(predicted_moments, 'stat', split_axis=1, concat_axis=0, ti...  3.08 us
  transfers between devices with their start and end apart: 2, of which 2 were waited for; matrix products, arithmetic and copies ran while one was open for 2% of the time, Pallas kernels for 0%

profile of v1, /device:TPU:0, one launch (start us, length us, event | category | flops | bytes accessed | tf_op | source)
XLA Modules:
  0.0 120.0 jit_solution(2143998904596616166)
XLA Ops:
  0.6 0.0 copy-start
  0.6 22.9 %all_to_all.45 = bf16[8,32,1024]{2,0,1:T(8,128)(2,1)S(1)} all-to-all(bf16[8,32,1024]{2,0,1:T(8,128)(2,1)} %bitcast.94), channel_id=1, replica_groups=mesh['groups'=1,'stat'=32] {'stat'}, dimensions={1} | all-to-all | bytes 1048576 | tf_op jit(solution)/shard_map/all_to_all | solution.py:270
  23.5 0.0 copy-start.1
  23.5 0.0 copy-start.3
  23.5 3.1 %all-to-all-start.1 = ((bf16[8,32,2048]{2,0,1:T(8,128)(2,1)}), bf16[8,32,2048]{2,0,1:T(8,128)(2,1)S(1)}, u32[]{:S(2)}, u32[]{:S(2)}) async-start(bf16[8,32,2048]{2,0,1:T(8,128)(2,1)} %bitcast.3), calls=%async_computation.1 | async-start | bytes 2097152 | tf_op jit(solution)/shard_map/all_to_all | solution.py:267
  26.6 0.0 copy-done.1
  26.6 0.1 add.101
  26.7 0.0 copy-done
  26.7 0.0 copy-done.3
  26.7 0.2 convolution_bitcast_fusion
  26.9 0.1 broadcast_bitcast_fusion
  27.7 0.1 convert_reduce_fusion.1
  27.8 25.0 %all-to-all-done.1 = bf16[8,32,2048]{2,0,1:T(8,128)(2,1)S(1)} async-done(((bf16[8,32,2048]{2,0,1:T(8,128)(2,1)}), bf16[8,32,2048]{2,0,1:T(8,128)(2,1)S(1)}, u32[]{:S(2)}, u32[]{:S(2)}) %all-to-all-start.1) | async-done | bytes 1048608 | tf_op jit(solution)/shard_map/all_to_all | solution.py:267
  52.8 0.2 convert_reduce_fusion
  53.0 0.0 copy-start.2
  53.0 0.6 fusion.116
  53.7 0.0 copy-done.2
  53.7 9.8 %fusion.63 = f32[256,256]{0,1:T(8,128)S(1)} fusion(bf16[8,32,2048]{2,0,1:T(8,128)(2,1)S(1)} %all-to-all-done.1, s32[2048]{0:T(1024)S(1)} %add_multiply_fusion, s32[32,8]{1,0:T(8,128)S(1)} %add.101, f32[2048]{0:T(1024)S(1)} %bitcast.96, f32[2048]{0:T(1024)S(1)} %copy-done.2, f32[2048]{0:T(1024)S(1)} %broadcast_multiply_fusion, ...), kind=kOutput, calls=%fused_computation.91 | convolution fusion | flops 287834112 | bytes 1352704 | tf_op jit(solution)/shard_map/dot_general | solution.py:43
  63.5 0.4 fusion.32
  63.9 5.1 %fusion.33 = f32[256,256]{0,1:T(8,128)S(1)} fusion(f32[256,256]{0,1:T(8,128)S(1)} %fusion.63, bf16[8,32,1024]{2,0,1:T(8,128)(2,1)S(1)} %all_to_all.45, s32[1024]{0:T(1024)S(1)} %add_multiply_fusion.1, s32[32,8]{1,0:T(8,128)S(1)} %add.101, f32[]{:T(128)} %bitcast.90, f32[1024]{0:T(1024)S(1)} %broadcast_multiply_fusion.2), kind=kOutput, calls=%fused_computation.60 | convolution fusion | flops 144048128 | bytes 1057796 | tf_op jit(solution)/shard_map/dot_general | solution.py:43
  69.1 0.1 pad_maximum_fusion
  69.1 0.2 copy.10
  69.3 21.9 %sum_over_devices.1 = f32[32,8,512]{2,1,0:T(8,128)S(1)} custom-call(f32[32,8,512]{2,1,0:T(8,128)S(1)} %bitcast.92), custom_call_target="tpu_custom_call" | custom-call | tf_op jit(solution)/shard_map/sum_over_devices/pallas_call | solution.py:155
  91.2 7.7 %solve_system.1 = bf16[256,256]{1,0:T(8,128)(2,1)S(1)} custom-call(f32[256,512]{1,0:T(8,128)S(1)} %bitcast.91), custom_call_target="tpu_custom_call" | custom-call | tf_op jit(solution)/shard_map/solve_system/pallas_call | solution.py:240
  99.0 1.1 fusion.31
  100.1 3.5 %all-to-all-start.2 = ((bf16[32,8,1024]{2,1,0:T(8,128)(2,1)}), bf16[32,8,1024]{2,1,0:T(8,128)(2,1)S(1)}, u32[]{:S(2)}, u32[]{:S(2)}) async-start(bf16[32,8,1024]{2,1,0:T(8,128)(2,1)} %fusion.31), calls=%async_computation.2 | async-start | bytes 1048576 | tf_op jit(solution)/shard_map/all_to_all | solution.py:303
  103.6 1.6 %fusion.2 = bf16[256,2048]{1,0:T(8,128)(2,1)} fusion(bf16[256,256]{1,0:T(8,128)(2,1)S(1)} %solve_system.1, bf16[8,32,2048]{2,0,1:T(8,128)(2,1)S(1)} %all-to-all-done.1, f32[2048]{0:T(1024)S(1)} %broadcast_multiply_fusion, f32[2048]{0:T(1024)S(1)} %broadcast_multiply_fusion.1, f32[2048]{0:T(1024)S(1)} %bitcast.97), kind=kOutput, calls=%fused_computation.15 | convolution fusion | flops 272629760 | bytes 2252800 | tf_op jit(solution)/shard_map/dot_general | solution.py:49
  105.2 14.0 %all-to-all-done.2 = bf16[32,8,1024]{2,1,0:T(8,128)(2,1)S(1)} async-done(((bf16[32,8,1024]{2,1,0:T(8,128)(2,1)}), bf16[32,8,1024]{2,1,0:T(8,128)(2,1)S(1)}, u32[]{:S(2)}, u32[]{:S(2)}) %all-to-all-start.2) | async-done | bytes 524320 | tf_op jit(solution)/shard_map/all_to_all | solution.py:303
  119.2 0.8 copy.14
  (7 shorter events, 0.0 us)
Async XLA Ops:
  0.6 26.1 %copy-start = (f32[24]{0:T(128)S(1)}, f32[24]{0:T(128)}, u32[]{:S(2)}) copy-start(f32[24]{0:T(128)} %param.11) | copy-start | bytes 292
  23.5 3.1 %copy-start.1 = (s32[256]{0:T(256)S(1)}, s32[256]{0:T(256)}, u32[]{:S(2)}) copy-start(s32[256]{0:T(256)} %param.13) | copy-start | bytes 3076
  23.5 3.2 %copy-start.3 = (s32[4]{0:T(128)S(1)}, s32[4]{0:T(128)}, u32[]{:S(2)}) copy-start(s32[4]{0:T(128)} %param.10) | copy-start | bytes 52
  23.5 29.3 %all-to-all-start.1 = ((bf16[8,32,2048]{2,0,1:T(8,128)(2,1)}), bf16[8,32,2048]{2,0,1:T(8,128)(2,1)S(1)}, u32[]{:S(2)}, u32[]{:S(2)}) async-start(bf16[8,32,2048]{2,0,1:T(8,128)(2,1)} %bitcast.3), calls=%async_computation.1 | async-start | bytes 2097152 | tf_op jit(solution)/shard_map/all_to_all | solution.py:267
  53.0 0.7 copy-start.2
  100.1 19.1 %all-to-all-start.2 = ((bf16[32,8,1024]{2,1,0:T(8,128)(2,1)}), bf16[32,8,1024]{2,1,0:T(8,128)(2,1)S(1)}, u32[]{:S(2)}, u32[]{:S(2)}) async-start(bf16[32,8,1024]{2,1,0:T(8,128)(2,1)} %fusion.31), calls=%async_computation.2 | async-start | bytes 1048576 | tf_op jit(solution)/shard_map/all_to_all | solution.py:303

commit v2 on v1

--- a/solution.py
+++ b/solution.py
@@ -32,11 +32,20 @@
     return (quotient.astype(jnp.float32) + 0.5) * 2.0 ** (-23)
 
 
-def normal_draw(member_random_keys, position):
-    hashed = member_random_keys[:, None] * seed_factor + position[None, :] * index_factor
+def sine_of_turns(turns):
+    square = turns * turns
+    value = jnp.float32(0.0)
+    for power in (11, 9, 7, 5, 3, 1):
+        sign = -1.0 if power % 4 == 3 else 1.0
+        value = value * square + sign * (2.0 * math.pi) ** power / math.factorial(power)
+    return value * turns
+
+
+def normal_from(hashed):
     first_part = uniform_from(hashed)
     second_part = uniform_from(hashed + 1)
-    return jnp.sqrt(-2.0 * jnp.log(first_part)) * jnp.cos(2.0 * math.pi * second_part)
+    radius = jnp.sqrt(jnp.maximum(-2.0 * jnp.log(first_part), 0.0))
+    return radius * sine_of_turns(jnp.abs(second_part - 0.5) - 0.25)
 
 
 def inner(left, right):
@@ -59,28 +68,28 @@
     return ((1, 2), (2, second), (2 * second, rest // second))
 
 
-def sum_kernel(stages, x_ref, o_ref, *scratch):
+def signal_peers(barrier, me, devices_total):
+    def signal(offset, carry):
+        pl.semaphore_signal(
+            barrier,
+            inc=1,
+            device_id={"stat": lax.rem(me + offset, devices_total)},
+            device_id_type=MESH,
+        )
+        return carry
+
+    lax.fori_loop(1, devices_total, signal, 0)
+    pl.semaphore_wait(barrier, devices_total - 1)
+
+
+def sum_stages(stages, me, x_ref, recvs, totals, gathered, send_sem, recv_sem, gsend_sem, grecv_sem):
     count = len(stages)
-    recvs = scratch[:count]
-    totals = scratch[count : 2 * count]
-    gathered, send_sem, recv_sem, gsend_sem, grecv_sem = scratch[2 * count :]
-    me = lax.axis_index("stat")
     digits = [lax.rem(lax.div(me, stride), size) for stride, size in stages]
 
     def peer(t, offset):
         stride, size = stages[t]
         other = lax.rem(digits[t] + offset, size)
         return other, me + (other - digits[t]) * stride
-
-    barrier = pltpu.get_barrier_semaphore()
-    peers = 0
-    for t, (stride, size) in enumerate(stages):
-        for offset in range(1, size):
-            pl.semaphore_signal(
-                barrier, inc=1, device_id={"stat": peer(t, offset)[1]}, device_id_type=MESH
-            )
-            peers += 1
-    pl.semaphore_wait(barrier, peers)
 
     source = x_ref
     length = x_ref.shape[0]
@@ -134,39 +143,245 @@
         for copy in copies:
             copy.wait()
         length *= size
-    o_ref[...] = gathered[...]
-
-
-def sum_over_devices(part, devices_total):
-    rows, columns = part.shape
-    chunks = max(rows // 8, devices_total)
-    spread = chunks // (rows // 8)
-    width = columns // spread
-    packed = part.reshape(rows // 8, 8, spread, width).transpose(0, 2, 1, 3)
-    packed = packed.reshape(chunks, 8, width)
+
+
+DRAW_ROWS = 8
+DRAW_LANES = 1024
+MIX = 13
+
+
+def exchange_kernel(
+    stages,
+    devices_total,
+    group_ref,
+    spread_of_group_ref,
+    prior_ref,
+    keys_ref,
+    measured_ref,
+    moments_ref,
+    vectors_ref,
+    total_ref,
+    closure_ref,
+    anomaly_ref,
+    params_ref,
+    spread_ref,
+    got_moments,
+    got_vectors,
+    draws,
+    part,
+    packed,
+    send_sem,
+    recv_sem,
+    own_sem,
+    *sum_scratch,
+):
+    me = lax.axis_index("stat")
+    members, stat_width = closure_ref.shape
+    par_width = params_ref.shape[1]
+    root_scale = math.sqrt(members - 1.0)
+    barrier = pltpu.get_barrier_semaphore()
+    signal_peers(barrier, me, devices_total)
+
+    def columns(device, width):
+        return pl.ds(pl.multiple_of(device * width, width), width)
+
+    kinds = ((moments_ref, got_moments, stat_width), (vectors_ref, got_vectors, par_width))
+
+    def copy_to(kind, step):
+        source, slots, width = kinds[kind]
+        device = lax.rem(me + lax.rem(step * MIX, devices_total), devices_total)
+        return pltpu.make_async_remote_copy(
+            src_ref=source.at[:, columns(device, width)],
+            dst_ref=slots.at[me],
+            send_sem=send_sem.at[kind, step],
+            recv_sem=recv_sem.at[kind, step],
+            device_id={"stat": device},
+            device_id_type=MESH,
+        )
+
+    def copy_from(kind, step):
+        source, slots, width = kinds[kind]
+        device = lax.rem(
+            me + devices_total - lax.rem(step * MIX, devices_total), devices_total
+        )
+        return pltpu.make_async_remote_copy(
+            src_ref=source.at[:, columns(me, width)],
+            dst_ref=slots.at[device],
+            send_sem=send_sem.at[kind, step],
+            recv_sem=recv_sem.at[kind, step],
+            device_id={"stat": device},
+            device_id_type=MESH,
+        )
+
+    own = []
+    for kind, (source, slots, width) in enumerate(kinds):
+
+        def start(step, carry, kind=kind):
+            copy_to(kind, step).start()
+            return carry
+
+        lax.fori_loop(1, devices_total, start, 0)
+        copy = pltpu.make_async_copy(
+            source.at[:, columns(me, width)], slots.at[me], own_sem.at[kind]
+        )
+        copy.start()
+        own.append(copy)
+
+    def wait_kind(kind):
+        def wait(step, carry):
+            copy_from(kind, step).wait_recv()
+            return carry
+
+        lax.fori_loop(1, devices_total, wait, 0)
+        own[kind].wait()
+
+    lane = lax.broadcasted_iota(jnp.int32, (DRAW_ROWS, DRAW_LANES), 1)
+    for first in range(0, stat_width + par_width, DRAW_LANES):
+        if first < stat_width:
+            position = me * stat_width + first
+        else:
+            position = devices_total * stat_width + me * par_width + (first - stat_width)
+        offsets = (lane + position) * index_factor
+
+        def draw(block, carry, first=first, offsets=offsets):
+            rows = pl.ds(pl.multiple_of(block * DRAW_ROWS, DRAW_ROWS), DRAW_ROWS)
+            hashed = keys_ref[rows, :] * seed_factor + offsets
+            draws[rows, first : first + DRAW_LANES] = normal_from(hashed)
+            return carry
+
+        lax.fori_loop(0, members // DRAW_ROWS, draw, 0)
+
+    wait_kind(0)
+    for slab in range(stat_width // SLAB):
+        here = slice(slab * SLAB, (slab + 1) * SLAB)
+        raw = got_moments[:, :, here].astype(jnp.float32).reshape(members, SLAB)
+        closure_ref[:, here] = raw.astype(jnp.bfloat16)
+        sigma = jnp.full((1, SLAB), spread_of_group_ref[group_ref[slab]], jnp.float32)
+        average = jnp.sum(raw, axis=0, keepdims=True) * (1.0 / members)
+        anomaly = ((raw - average) * (1.0 / (sigma * root_scale))).astype(jnp.bfloat16)
+        anomaly_ref[:, here] = anomaly
+        misfit = (
+            (measured_ref[:, here] - raw) * (1.0 / sigma) + draws[:, here]
+        ).astype(jnp.bfloat16)
+        product = inner(anomaly, jnp.concatenate([anomaly, misfit], axis=0))
+        part[...] = product if slab == 0 else part[...] + product
+
+    wait_kind(1)
+    prior = jnp.full((1, SLAB), prior_ref[0], jnp.float32)
+    prior_inverse = 1.0 / prior
+    lanes = lax.broadcasted_iota(jnp.int32, (1, 2 * members), 1)
+    prior_members = jnp.full((1, 2 * members), prior_ref[0], jnp.float32)
+    scale = 1.0 / jnp.where(lanes < members, prior_members * prior_members, prior_members)
+    for slab in range(par_width // SLAB):
+        here = slice(slab * SLAB, (slab + 1) * SLAB)
+        raw = got_vectors[:, :, here].astype(jnp.float32).reshape(members, SLAB)
+        params_ref[:, here] = raw.astype(jnp.bfloat16)
+        average = jnp.sum(raw, axis=0, keepdims=True) * (1.0 / members)
+        spread = ((raw - average) * (1.0 / root_scale)).astype(jnp.bfloat16)
+        spread_ref[:, here] = spread
+        drawn = draws[:, stat_width + slab * SLAB : stat_width + (slab + 1) * SLAB]
+        misfit = (drawn - raw * prior_inverse).astype(jnp.bfloat16)
+        product = inner(spread, jnp.concatenate([spread, misfit], axis=0))
+        part[...] += product * scale
+
+    chunks, _, width = packed.shape
+    fold = (2 * members) // width
+    if fold == 1:
+        packed[...] = part[...].reshape(packed.shape)
+    else:
+        for chunk in range(chunks):
+            low, side = chunk // fold * 8, chunk % fold * width
+            packed[chunk] = part[low : low + 8, side : side + width]
+    gathered = sum_scratch[2 * len(stages)]
+    sum_stages(
+        stages,
+        me,
+        packed,
+        sum_scratch[: len(stages)],
+        sum_scratch[len(stages) : 2 * len(stages)],
+        gathered,
+        *sum_scratch[2 * len(stages) + 1 :],
+    )
+    if fold == 1:
+        total_ref[...] = gathered[...].reshape(total_ref.shape)
+    else:
+        for chunk in range(chunks):
+            low, side = chunk // fold * 8, chunk % fold * width
+            total_ref[low : low + 8, side : side + width] = gathered[chunk]
+
+    def wait_sent(step, carry):
+        copy_to(0, step).wait_send()
+        copy_to(1, step).wait_send()
+        return carry
+
+    lax.fori_loop(1, devices_total, wait_sent, 0)
+
+
+def exchange(
+    predicted_moments,
+    member_vectors,
+    measured_moments,
+    block_error_group,
+    group_error_spread,
+    background_spread,
+    member_random_keys,
+    devices_total,
+):
+    each, all_moments = predicted_moments.shape
+    stat_width = all_moments // devices_total
+    par_width = member_vectors.shape[1] // devices_total
+    members = each * devices_total
+    chunks = max(members // 8, devices_total)
+    packed = (chunks, 8, members // 8 * 2 * members // chunks)
     stages = stages_of(devices_total)
     recvs, totals, length, copies = [], [], chunks, 0
     for stride, size in stages:
         length //= size
-        recvs.append(pltpu.VMEM((size - 1, length, 8, width), jnp.float32))
-        totals.append(pltpu.VMEM((length, 8, width), jnp.float32))
+        recvs.append(pltpu.VMEM((size - 1, length) + packed[1:], jnp.float32))
+        totals.append(pltpu.VMEM((length,) + packed[1:], jnp.float32))
         copies += size - 1
-    whole = pl.BlockSpec(memory_space=pltpu.VMEM)
-    out = pl.pallas_call(
-        functools.partial(sum_kernel, stages),
-        out_shape=jax.ShapeDtypeStruct(packed.shape, jnp.float32),
-        in_specs=[whole],
-        out_specs=whole,
-        scratch_shapes=recvs
+    vmem = pl.BlockSpec(memory_space=pltpu.VMEM)
+    smem = pl.BlockSpec(memory_space=pltpu.SMEM)
+    anywhere = pl.BlockSpec(memory_space=pl.ANY)
+    shape = jax.ShapeDtypeStruct
+    return pl.pallas_call(
+        functools.partial(exchange_kernel, stages, devices_total),
+        out_shape=(
+            shape((members, 2 * members), jnp.float32),
+            shape((members, stat_width), jnp.bfloat16),
+            shape((members, stat_width), jnp.bfloat16),
+            shape((members, par_width), jnp.bfloat16),
+            shape((members, par_width), jnp.bfloat16),
+        ),
+        in_specs=[smem, smem, smem, vmem, vmem, anywhere, anywhere],
+        out_specs=(vmem,) * 5,
+        scratch_shapes=[
+            pltpu.VMEM((devices_total, each, stat_width), jnp.bfloat16),
+            pltpu.VMEM((devices_total, each, par_width), jnp.bfloat16),
+            pltpu.VMEM((members, stat_width + par_width), jnp.float32),
+            pltpu.VMEM((members, 2 * members), jnp.float32),
+            pltpu.VMEM(packed, jnp.float32),
+            pltpu.SemaphoreType.DMA((2, devices_total)),
+            pltpu.SemaphoreType.DMA((2, devices_total)),
+            pltpu.SemaphoreType.DMA((2,)),
+        ]
+        + recvs
         + totals
-        + [pltpu.VMEM(packed.shape, jnp.float32)]
+        + [pltpu.VMEM(packed, jnp.float32)]
         + [pltpu.SemaphoreType.DMA((copies,))] * 4,
         compiler_params=pltpu.CompilerParams(
-            collective_id=0, has_side_effects=True, vmem_limit_bytes=16 * 2**20
+            collective_id=0, has_side_effects=True, vmem_limit_bytes=40 * 2**20
         ),
-        name="sum_over_devices",
-    )(packed)
-    return out.reshape(rows // 8, spread, 8, width).transpose(0, 2, 1, 3).reshape(rows, columns)
+        name="exchange",
+    )(
+        block_error_group,
+        group_error_spread,
+        background_spread,
+        member_random_keys[:, None],
+        measured_moments[None, :],
+        predicted_moments,
+        member_vectors,
+    )
 
 
 def exact_dot(left, right):
@@ -258,16 +473,17 @@
     member_random_keys,
 ):
     devices_total = lax.axis_size("stat")
-    device_rank = lax.axis_index("stat")
     stat_width = measured_moments.shape[0]
-    par_width = member_vectors.shape[1] // devices_total
-    members = member_random_keys.shape[0]
-    root_scale = math.sqrt(members - 1.0)
-    prior = background_spread[0]
-    shard_result_lines = lax.all_to_all(
-        predicted_moments, "stat", split_axis=1, concat_axis=0, tiled=True
-    )
-    params_rows = lax.all_to_all(member_vectors, "stat", split_axis=1, concat_axis=0, tiled=True)
+    total, closure, anomaly, params, spread = exchange(
+        predicted_moments,
+        member_vectors,
+        measured_moments,
+        block_error_group,
+        group_error_spread,
+        background_spread,
+        member_random_keys,
+        devices_total,
+    )
     classes = group_error_spread.shape[0]
     selector = (block_error_group[:, None] == jnp.arange(classes, dtype=jnp.int32)[None, :]).astype(
         jnp.float32
@@ -276,34 +492,14 @@
     sigma = jnp.broadcast_to(slab_sigma[:, None], (block_error_group.shape[0], SLAB)).reshape(
         stat_width
     )
-    closure_results = shard_result_lines.astype(jnp.float32)
-    out_average = jnp.mean(closure_results, axis=0)
-    anomaly = ((closure_results - out_average) / (sigma * root_scale)).astype(jnp.bfloat16)
-    stat_position = device_rank * stat_width + jnp.arange(stat_width, dtype=jnp.int32)
-    misfit = (
-        (measured_moments - closure_results) / sigma
-        + normal_draw(member_random_keys, stat_position)
+    weights = solve_system(total)
+    updated_rows = (
+        params.astype(jnp.float32) + transposed_product(weights, spread)
     ).astype(jnp.bfloat16)
-    params = params_rows.astype(jnp.float32)
-    par_average = jnp.mean(params, axis=0)
-    spread = ((params - par_average) / root_scale).astype(jnp.bfloat16)
-    par_position = (
-        devices_total * stat_width
-        + device_rank * par_width
-        + jnp.arange(par_width, dtype=jnp.int32)
-    )
-    prior_misfit = (-params / prior + normal_draw(member_random_keys, par_position)).astype(
-        jnp.bfloat16
-    )
-    gram_part = inner(anomaly, anomaly) + inner(spread, spread) / (prior * prior)
-    cross_part = inner(anomaly, misfit) + inner(spread, prior_misfit) / prior
-    total = sum_over_devices(jnp.concatenate([gram_part, cross_part], axis=1), devices_total)
-    weights = solve_system(total)
-    updated_rows = (params + transposed_product(weights, spread)).astype(jnp.bfloat16)
     updated = lax.all_to_all(updated_rows, "stat", split_axis=0, concat_axis=1, tiled=True)
-    predicted = (closure_results + sigma[None, :] * transposed_product(weights, anomaly)).astype(
-        jnp.bfloat16
-    )
+    predicted = (
+        closure.astype(jnp.float32) + sigma[None, :] * transposed_product(weights, anomaly)
+    ).astype(jnp.bfloat16)
     return (updated, predicted)
 
 

time: 120 us -> 100 us (0.83)
  Pallas kernels: 29.6 us -> 72.6 us
  waiting for transfers between devices: 39 us -> 13.8 us
  blocking collectives: 22.9 us -> 0 us
  matrix products: 18.9 us -> 2.75 us
  local copies, waits for them, and re-layouts: 1.22 us -> 5.96 us
  starting transfers between devices: 6.6 us -> 3.49 us
    pallas_call x1, Pallas kernels: 21.9 us -> 64.9 us  [exchange(): pl.pallas_call(functools.partial(exchange_kernel, stages, devices_total),...]
    all_to_all x1 -> x0, waiting for transfers between devices: 25 us -> none  [body(): lax.all_to_all(predicted_moments, 'stat', split_axis=1, concat_axis=0, ti...]
    all_to_all x1 -> x0, blocking collectives: 22.9 us -> none  [body(): lax.all_to_all(member_vectors, 'stat', split_axis=1, concat_axis=0, tiled...]
    dot_general x4 -> x0, matrix products: 16 us -> none  [inner(): lax.dot_general(left, right, (((1,), (1,)), ((), ())), preferred_element_...]
    unnamed x11 -> x17, local copies, waits for them, and re-layouts: 0.94 us -> 5.15 us
    all_to_all x1 -> x0, starting transfers between devices: 3.08 us -> none  [body(): lax.all_to_all(predicted_moments, 'stat', split_axis=1, concat_axis=0, ti...]
  transfers between devices with their start and end apart: 2 -> 1, of which waited for: 2 -> 1; matrix products, arithmetic and copies ran while one was open for 2% -> 2% of each run, Pallas kernels for 0% -> 0%
where the time goes in v2:
time: 100 us
  Pallas kernels  72.6 us (73%)
  waiting for transfers between devices  13.8 us (14%)
  local copies, waits for them, and re-layouts  5.96 us (6%)
  starting transfers between devices  3.49 us (3%)
  matrix products  2.75 us (3%)
  between operations  1.35 us (1%)
    pallas_call x1, Pallas kernels, exchange(): pl.pallas_call(functools.partial(exchange_kernel, stages, devices_total),...  64.9 us
    all_to_all x1, waiting for transfers between devices, body(): lax.all_to_all(updated_rows, 'stat', split_axis=0, concat_axis=1, tiled=T...  13.8 us
    pallas_call x1, Pallas kernels, solve_system(): pl.pallas_call(solve_kernel, out_shape=jax.ShapeDtypeStruct((size, total....  7.72 us
    unnamed x17, local copies, waits for them, and re-layouts  5.15 us
    all_to_all x1, starting transfers between devices, body(): lax.all_to_all(updated_rows, 'stat', split_axis=0, concat_axis=1, tiled=T...  3.49 us
    dot_general x2, matrix products, transposed_product(): lax.dot_general(weights, right, (((0,), (0,)), ((), ())), preferred_eleme...  2.56 us
  transfers between devices with their start and end apart: 1, of which 1 were waited for; matrix products, arithmetic and copies ran while one was open for 2% of the time, Pallas kernels for 0%

profile of v2, /device:TPU:0, one launch (start us, length us, event | category | flops | bytes accessed | tf_op | source)
XLA Modules:
  0.0 100.0 jit_solution(8438774529051223700)
XLA Ops:
  1.3 0.8 copy.9.keys_ref
  2.1 0.0 copy-start
  2.1 1.2 %copy-done = bf16[8,65536]{1,0:T(8,128)(2,1)S(1)} copy-done((bf16[8,65536]{1,0:T(8,128)(2,1)S(1)}, bf16[8,65536]{1,0:T(8,128)(2,1)}, u32[]{:S(2)}) %copy-start) | copy-done | bytes 1048600
  3.3 0.0 copy-start.1
  3.3 1.0 %copy-done.1 = bf16[8,32768]{1,0:T(8,128)(2,1)S(1)} copy-done((bf16[8,32768]{1,0:T(8,128)(2,1)S(1)}, bf16[8,32768]{1,0:T(8,128)(2,1)}, u32[]{:S(2)}) %copy-start.1) | copy-done | bytes 524312
  4.4 0.0 copy-start.2
  4.4 0.7 copy-done.2
  5.1 0.0 copy-start.3
  5.1 0.7 copy-done.3
  5.7 0.0 copy-start.5
  5.7 0.7 copy-done.5
  6.4 64.9 %exchange.1 = (f32[256,512]{1,0:T(8,128)S(1)}, bf16[256,2048]{1,0:T(8,128)(2,1)S(1)}, bf16[256,2048]{1,0:T(8,128)(2,1)S(1)}, bf16[256,1024]{1,0:T(8,128)(2,1)S(1)}, bf16[256,1024]{1,0:T(8,128)(2,1)S(1)}) custom-call(s32[4]{0:T(128)S(1)} %copy-done.3, f32[24]{0:T(128)S(1)} %copy-done.5, f32[1]{0:T(128)S(6)} %copy.12.prior_ref, s32[256,1]{1,0:T(8,128)S(1)} %copy.9.keys_ref, ...), custom_call_target="tpu_custom_call" | custom-call | tf_op jit(solution)/shard_map/exchange/pallas_call | solution.py:347
  71.3 7.7 %solve_system.1 = bf16[256,256]{1,0:T(8,128)(2,1)S(1)} custom-call(f32[256,512]{1,0:T(8,128)S(1)} %get-tuple-element.8.s_ref), custom_call_target="tpu_custom_call" | custom-call | tf_op jit(solution)/shard_map/solve_system/pallas_call | solution.py:455
  79.0 0.0 copy-start.4
  79.0 0.0 copy-start.6
  79.0 1.1 %fusion.3 = bf16[32,8,1024]{2,1,0:T(8,128)(2,1)} fusion(bf16[256,256]{1,0:T(8,128)(2,1)S(1)} %solve_system.1, bf16[256,1024]{1,0:T(8,128)(2,1)S(1)} %get-tuple-element.9, bf16[256,1024]{1,0:T(8,128)(2,1)S(1)} %get-tuple-element.7), kind=kOutput, calls=%fused_computation.5 | convolution fusion | flops 135004160 | bytes 1703936 | tf_op jit(solution)/shard_map/dot_general | solution.py:58
  80.1 3.5 %all-to-all-start = ((bf16[32,8,1024]{2,1,0:T(8,128)(2,1)}), bf16[32,8,1024]{2,1,0:T(8,128)(2,1)S(1)}, u32[]{:S(2)}, u32[]{:S(2)}) async-start(bf16[32,8,1024]{2,1,0:T(8,128)(2,1)} %fusion.3), calls=%async_computation | async-start | bytes 1048576 | tf_op jit(solution)/shard_map/all_to_all | solution.py:499
  83.6 0.0 copy-done.4
  83.6 0.0 copy-done.6
  83.6 0.2 convolution_bitcast_fusion
  83.8 0.1 broadcast_bitcast_fusion
  83.9 1.4 %fusion.1 = bf16[256,2048]{1,0:T(8,128)(2,1)} fusion(bf16[256,256]{1,0:T(8,128)(2,1)S(1)} %solve_system.1, bf16[256,2048]{1,0:T(8,128)(2,1)S(1)} %get-tuple-element.11, bf16[256,2048]{1,0:T(8,128)(2,1)S(1)} %get-tuple-element.10, f32[2048]{0:T(1024)S(1)} %bitcast.21), kind=kOutput, calls=%fused_computation.2 | convolution fusion | flops 270532608 | bytes 3284992 | tf_op jit(solution)/shard_map/dot_general | solution.py:58
  85.4 13.8 %all-to-all-done = bf16[32,8,1024]{2,1,0:T(8,128)(2,1)S(1)} async-done(((bf16[32,8,1024]{2,1,0:T(8,128)(2,1)}), bf16[32,8,1024]{2,1,0:T(8,128)(2,1)S(1)}, u32[]{:S(2)}, u32[]{:S(2)}) %all-to-all-start) | async-done | bytes 524320 | tf_op jit(solution)/shard_map/all_to_all | solution.py:499
  99.2 0.8 copy.13
  (1 shorter events, 0.0 us)
Async XLA Ops:
  2.1 1.2 %copy-start = (bf16[8,65536]{1,0:T(8,128)(2,1)S(1)}, bf16[8,65536]{1,0:T(8,128)(2,1)}, u32[]{:S(2)}) copy-start(bf16[8,65536]{1,0:T(8,128)(2,1)} %moments_ref.1) | copy-start | bytes 3145732
  3.3 1.0 %copy-start.1 = (bf16[8,32768]{1,0:T(8,128)(2,1)S(1)}, bf16[8,32768]{1,0:T(8,128)(2,1)}, u32[]{:S(2)}) copy-start(bf16[8,32768]{1,0:T(8,128)(2,1)} %vectors_ref.1) | copy-start | bytes 1572868
  4.4 0.7 copy-start.2
  5.1 0.7 copy-start.3
  5.7 0.7 copy-start.5
  79.0 4.6 %copy-start.4 = (s32[4]{0:T(128)S(1)}, s32[4]{0:T(128)}, u32[]{:S(2)}) copy-start(s32[4]{0:T(128)} %group_ref.1) | copy-start | bytes 52
  79.0 4.6 %copy-start.6 = (f32[24]{0:T(128)S(1)}, f32[24]{0:T(128)}, u32[]{:S(2)}) copy-start(f32[24]{0:T(128)} %spread_of_group_ref.1) | copy-start | bytes 292
  80.1 19.0 %all-to-all-start = ((bf16[32,8,1024]{2,1,0:T(8,128)(2,1)}), bf16[32,8,1024]{2,1,0:T(8,128)(2,1)S(1)}, u32[]{:S(2)}, u32[]{:S(2)}) async-start(bf16[32,8,1024]{2,1,0:T(8,128)(2,1)} %fusion.3), calls=%async_computation | async-start | bytes 1048576 | tf_op jit(solution)/shard_map/all_to_all | solution.py:499

commit v3 on v2

--- a/solution.py
+++ b/solution.py
@@ -51,12 +51,6 @@
 def inner(left, right):
     return lax.dot_general(
         left, right, (((1,), (1,)), ((), ())), preferred_element_type=jnp.float32
-    )
-
-
-def transposed_product(weights, right):
-    return lax.dot_general(
-        weights, right, (((0,), (0,)), ((), ())), preferred_element_type=jnp.float32
     )
 
 
@@ -79,70 +73,86 @@
         return carry
 
     lax.fori_loop(1, devices_total, signal, 0)
-    pl.semaphore_wait(barrier, devices_total - 1)
-
-
-def sum_stages(stages, me, x_ref, recvs, totals, gathered, send_sem, recv_sem, gsend_sem, grecv_sem):
+
+
+def sum_stages(stages, me, packed, recvs, totals, gathered, send_sem, recv_sem, gsend_sem, grecv_sem):
     count = len(stages)
+    ways, chunks = packed.shape[:2]
     digits = [lax.rem(lax.div(me, stride), size) for stride, size in stages]
+    lengths, bases, slots = [chunks], [0], [0]
+    for t, (stride, size) in enumerate(stages):
+        lengths.append(lengths[t] // size)
+        bases.append(bases[t] + digits[t] * lengths[t + 1])
+        slots.append(slots[t] + size - 1)
 
     def peer(t, offset):
         stride, size = stages[t]
         other = lax.rem(digits[t] + offset, size)
         return other, me + (other - digits[t]) * stride
 
-    source = x_ref
-    length = x_ref.shape[0]
-    bases = [0]
-    slot = 0
-    for t, (stride, size) in enumerate(stages):
-        piece = length // size
+    def source(t, way):
+        return packed.at[way] if t == 0 else totals[t - 1].at[way]
+
+    def start_scatter(t, way):
         copies = []
-        for offset in range(1, size):
+        for offset in range(1, stages[t][1]):
             other, device = peer(t, offset)
+            slot = slots[t] + offset - 1
             copy = pltpu.make_async_remote_copy(
-                src_ref=source.at[pl.ds(other * piece, piece)],
-                dst_ref=recvs[t].at[offset - 1],
-                send_sem=send_sem.at[slot],
-                recv_sem=recv_sem.at[slot],
+                src_ref=source(t, way).at[pl.ds(other * lengths[t + 1], lengths[t + 1])],
+                dst_ref=recvs[t].at[way, offset - 1],
+                send_sem=send_sem.at[way, slot],
+                recv_sem=recv_sem.at[way, slot],
                 device_id={"stat": device},
                 device_id_type=MESH,
             )
             copy.start()
             copies.append(copy)
-            slot += 1
-        value = source[pl.ds(digits[t] * piece, piece)]
-        for offset in range(1, size):
-            copies[offset - 1].wait_recv()
-            value = value + recvs[t][offset - 1]
-        totals[t][...] = value
-        for copy in copies:
-            copy.wait_send()
-        bases.append(bases[t] + digits[t] * piece)
-        source, length = totals[t], piece
-
-    gathered[pl.ds(bases[count], length)] = source[...]
-    slot = 0
-    for t in reversed(range(count)):
-        stride, size = stages[t]
+        return copies
+
+    def start_gather(t, way):
         copies = []
-        for offset in range(1, size):
+        for offset in range(1, stages[t][1]):
             _, device = peer(t, offset)
-            own = gathered.at[pl.ds(bases[t + 1], length)]
+            slot = slots[t] + offset - 1
+            own = gathered.at[way, pl.ds(bases[t + 1], lengths[t + 1])]
             copy = pltpu.make_async_remote_copy(
                 src_ref=own,
                 dst_ref=own,
-                send_sem=gsend_sem.at[slot],
-                recv_sem=grecv_sem.at[slot],
+                send_sem=gsend_sem.at[way, slot],
+                recv_sem=grecv_sem.at[way, slot],
                 device_id={"stat": device},
                 device_id_type=MESH,
             )
             copy.start()
             copies.append(copy)
-            slot += 1
-        for copy in copies:
-            copy.wait()
-        length *= size
+        return copies
+
+    flying = [start_scatter(0, way) for way in range(ways)]
+    sent = []
+    for t in range(count):
+        for way in range(ways):
+            copies = flying[way]
+            value = source(t, way)[pl.ds(digits[t] * lengths[t + 1], lengths[t + 1])]
+            for offset, copy in enumerate(copies):
+                copy.wait_recv()
+                value = value + recvs[t][way, offset]
+            sent += copies
+            if t + 1 < count:
+                totals[t][way] = value
+                flying[way] = start_scatter(t + 1, way)
+            else:
+                gathered[way, pl.ds(bases[count], lengths[count])] = value
+                flying[way] = start_gather(t, way)
+    for t in reversed(range(count)):
+        for way in range(ways):
+            for copy in flying[way]:
+                copy.wait_recv()
+            sent += flying[way]
+            if t > 0:
+                flying[way] = start_gather(t - 1, way)
+    for copy in sent:
+        copy.wait_send()
 
 
 DRAW_ROWS = 8
@@ -153,34 +163,58 @@
 def exchange_kernel(
     stages,
     devices_total,
+    group_hbm,
+    spread_of_group_hbm,
+    prior_hbm,
+    keys_hbm,
+    measured_hbm,
+    moments_ref,
+    vectors_ref,
+    total_ref,
+    closure_hbm,
+    anomaly_hbm,
+    params_hbm,
+    spread_hbm,
     group_ref,
     spread_of_group_ref,
     prior_ref,
+    keys_row,
     keys_ref,
     measured_ref,
-    moments_ref,
-    vectors_ref,
-    total_ref,
-    closure_ref,
-    anomaly_ref,
-    params_ref,
-    spread_ref,
     got_moments,
     got_vectors,
+    anomaly_ref,
+    spread_ref,
     draws,
     part,
     packed,
     send_sem,
     recv_sem,
     own_sem,
+    small_sem,
+    out_sem,
     *sum_scratch,
 ):
     me = lax.axis_index("stat")
-    members, stat_width = closure_ref.shape
-    par_width = params_ref.shape[1]
+    members, stat_width = anomaly_ref.shape
+    par_width = spread_ref.shape[1]
     root_scale = math.sqrt(members - 1.0)
     barrier = pltpu.get_barrier_semaphore()
     signal_peers(barrier, me, devices_total)
+    small = []
+    for index, (source, target) in enumerate(
+        (
+            (keys_hbm, keys_row),
+            (measured_hbm, measured_ref),
+            (group_hbm, group_ref),
+            (spread_of_group_hbm, spread_of_group_ref),
+            (prior_hbm, prior_ref),
+        )
+    ):
+        copy = pltpu.make_async_copy(source, target, small_sem.at[index])
+        copy.start()
+        small.append(copy)
+    pl.semaphore_wait(barrier, devices_total - 1)
 
     def columns(device, width):
         return pl.ds(pl.multiple_of(device * width, width), width)
@@ -235,6 +269,11 @@
         lax.fori_loop(1, devices_total, wait, 0)
         own[kind].wait()
 
+    for copy in small:
+        copy.wait()
+    for low in range(0, members, LANES):
+        keys = jnp.broadcast_to(keys_row[:, low : low + LANES], (LANES, LANES))
+        keys_ref[low : low + LANES, :] = keys.T * seed_factor
     lane = lax.broadcasted_iota(jnp.int32, (DRAW_ROWS, DRAW_LANES), 1)
     for first in range(0, stat_width + par_width, DRAW_LANES):
         if first < stat_width:
@@ -245,17 +284,25 @@
 
         def draw(block, carry, first=first, offsets=offsets):
             rows = pl.ds(pl.multiple_of(block * DRAW_ROWS, DRAW_ROWS), DRAW_ROWS)
-            hashed = keys_ref[rows, :] * seed_factor + offsets
+            seeds = jnp.concatenate([keys_ref[rows, :]] * (DRAW_LANES // LANES), axis=1)
+            hashed = seeds + offsets
             draws[rows, first : first + DRAW_LANES] = normal_from(hashed)
             return carry
 
         lax.fori_loop(0, members // DRAW_ROWS, draw, 0)
 
+    outgoing = []
+
+    def send_out(source, target):
+        copy = pltpu.make_async_copy(source, target, out_sem.at[len(outgoing)])
+        copy.start()
+        outgoing.append(copy)
+
     wait_kind(0)
+    send_out(got_moments, closure_hbm)
     for slab in range(stat_width // SLAB):
         here = slice(slab * SLAB, (slab + 1) * SLAB)
         raw = got_moments[:, :, here].astype(jnp.float32).reshape(members, SLAB)
-        closure_ref[:, here] = raw.astype(jnp.bfloat16)
         sigma = jnp.full((1, SLAB), spread_of_group_ref[group_ref[slab]], jnp.float32)
         average = jnp.sum(raw, axis=0, keepdims=True) * (1.0 / members)
         anomaly = ((raw - average) * (1.0 / (sigma * root_scale))).astype(jnp.bfloat16)
@@ -266,7 +313,9 @@
         product = inner(anomaly, jnp.concatenate([anomaly, misfit], axis=0))
         part[...] = product if slab == 0 else part[...] + product
 
+    send_out(anomaly_ref, anomaly_hbm)
     wait_kind(1)
+    send_out(got_vectors, params_hbm)
     prior = jnp.full((1, SLAB), prior_ref[0], jnp.float32)
     prior_inverse = 1.0 / prior
     lanes = lax.broadcasted_iota(jnp.int32, (1, 2 * members), 1)
@@ -275,7 +324,6 @@
     for slab in range(par_width // SLAB):
         here = slice(slab * SLAB, (slab + 1) * SLAB)
         raw = got_vectors[:, :, here].astype(jnp.float32).reshape(members, SLAB)
-        params_ref[:, here] = raw.astype(jnp.bfloat16)
         average = jnp.sum(raw, axis=0, keepdims=True) * (1.0 / members)
         spread = ((raw - average) * (1.0 / root_scale)).astype(jnp.bfloat16)
         spread_ref[:, here] = spread
@@ -284,15 +332,19 @@
         product = inner(spread, jnp.concatenate([spread, misfit], axis=0))
         part[...] += product * scale
 
-    chunks, _, width = packed.shape
-    fold = (2 * members) // width
-    if fold == 1:
-        packed[...] = part[...].reshape(packed.shape)
-    else:
-        for chunk in range(chunks):
-            low, side = chunk // fold * 8, chunk % fold * width
-            packed[chunk] = part[low : low + 8, side : side + width]
+    send_out(spread_ref, spread_hbm)
+    ways, chunks, _, width = packed.shape
     gathered = sum_scratch[2 * len(stages)]
+    fold = (2 * members) // (width * ways)
+    for way in range(ways):
+        for side in range(fold):
+            here = slice((way * fold + side) * width, (way * fold + side + 1) * width)
+            block = part[:, here].reshape(members // 8, 8, width)
+            if fold == 1:
+                packed[way] = block
+            else:
+                for low in range(members // 8):
+                    packed[way, low * fold + side] = block[low]
     sum_stages(
         stages,
         me,
@@ -302,12 +354,16 @@
         gathered,
         *sum_scratch[2 * len(stages) + 1 :],
     )
-    if fold == 1:
-        total_ref[...] = gathered[...].reshape(total_ref.shape)
-    else:
-        for chunk in range(chunks):
-            low, side = chunk // fold * 8, chunk % fold * width
-            total_ref[low : low + 8, side : side + width] = gathered[chunk]
+    for way in range(ways):
+        for side in range(fold):
+            here = slice((way * fold + side) * width, (way * fold + side + 1) * width)
+            if fold == 1:
+                total_ref[:, here] = gathered[way].reshape(members, width)
+            else:
+                for low in range(members // 8):
+                    total_ref[low * 8 : low * 8 + 8, here] = gathered[way, low * fold + side]
+    for copy in outgoing:
+        copy.wait()
 
     def wait_sent(step, carry):
         copy_to(0, step).wait_send()
@@ -332,43 +388,54 @@
     par_width = member_vectors.shape[1] // devices_total
     members = each * devices_total
     chunks = max(members // 8, devices_total)
-    packed = (chunks, 8, members // 8 * 2 * members // chunks)
+    width = members // 8 * 2 * members // chunks
+    ways = 2 if width == 2 * members else 1
+    packed = (ways, chunks, 8, width // ways)
     stages = stages_of(devices_total)
     recvs, totals, length, copies = [], [], chunks, 0
     for stride, size in stages:
         length //= size
-        recvs.append(pltpu.VMEM((size - 1, length) + packed[1:], jnp.float32))
-        totals.append(pltpu.VMEM((length,) + packed[1:], jnp.float32))
+        recvs.append(pltpu.VMEM((ways, size - 1, length) + packed[2:], jnp.float32))
+        totals.append(pltpu.VMEM((ways, length) + packed[2:], jnp.float32))
         copies += size - 1
     vmem = pl.BlockSpec(memory_space=pltpu.VMEM)
-    smem = pl.BlockSpec(memory_space=pltpu.SMEM)
-    anywhere = pl.BlockSpec(memory_space=pl.ANY)
+    hbm = pl.BlockSpec(memory_space=pltpu.HBM)
     shape = jax.ShapeDtypeStruct
     return pl.pallas_call(
         functools.partial(exchange_kernel, stages, devices_total),
         out_shape=(
             shape((members, 2 * members), jnp.float32),
+            shape((devices_total, each, stat_width), jnp.bfloat16),
             shape((members, stat_width), jnp.bfloat16),
-            shape((members, stat_width), jnp.bfloat16),
-            shape((members, par_width), jnp.bfloat16),
+            shape((devices_total, each, par_width), jnp.bfloat16),
             shape((members, par_width), jnp.bfloat16),
         ),
-        in_specs=[smem, smem, smem, vmem, vmem, anywhere, anywhere],
-        out_specs=(vmem,) * 5,
+        in_specs=[hbm] * 7,
+        out_specs=(vmem, hbm, hbm, hbm, hbm),
         scratch_shapes=[
+            pltpu.SMEM(block_error_group.shape, jnp.int32),
+            pltpu.SMEM(group_error_spread.shape, jnp.float32),
+            pltpu.SMEM(background_spread.shape, jnp.float32),
+            pltpu.VMEM((1, members), jnp.int32),
+            pltpu.VMEM((members, LANES), jnp.int32),
+            pltpu.VMEM((1, stat_width), jnp.float32),
             pltpu.VMEM((devices_total, each, stat_width), jnp.bfloat16),
             pltpu.VMEM((devices_total, each, par_width), jnp.bfloat16),
+            pltpu.VMEM((members, stat_width), jnp.bfloat16),
+            pltpu.VMEM((members, par_width), jnp.bfloat16),
             pltpu.VMEM((members, stat_width + par_width), jnp.float32),
             pltpu.VMEM((members, 2 * members), jnp.float32),
             pltpu.VMEM(packed, jnp.float32),
             pltpu.SemaphoreType.DMA((2, devices_total)),
             pltpu.SemaphoreType.DMA((2, devices_total)),
             pltpu.SemaphoreType.DMA((2,)),
+            pltpu.SemaphoreType.DMA((5,)),
+            pltpu.SemaphoreType.DMA((4,)),
         ]
         + recvs
         + totals
         + [pltpu.VMEM(packed, jnp.float32)]
-        + [pltpu.SemaphoreType.DMA((copies,))] * 4,
+        + [pltpu.SemaphoreType.DMA((ways, copies))] * 4,
         compiler_params=pltpu.CompilerParams(
             collective_id=0, has_side_effects=True, vmem_limit_bytes=40 * 2**20
         ),
@@ -377,7 +444,7 @@
         block_error_group,
         group_error_spread,
         background_spread,
-        member_random_keys[:, None],
+        member_random_keys[None, :],
         measured_moments[None, :],
         predicted_moments,
         member_vectors,
@@ -446,7 +513,7 @@
                 left[low:high], right
             )
         m_ref[start:after, from_column:] = top
-    w_ref[...] = m_ref[:, size:].astype(w_ref.dtype)
+    w_ref[...] = m_ref[:, size:].T.astype(w_ref.dtype)
 
 
 def solve_system(total):
@@ -463,6 +530,103 @@
     )(total)
 
 
+def update_kernel(
+    devices_total,
+    group_ref,
+    spread_of_group_ref,
+    weights_ref,
+    closure_ref,
+    anomaly_ref,
+    params_ref,
+    spread_ref,
+    updated_ref,
+    predicted_ref,
+    rows,
+    send_sem,
+    recv_sem,
+    own_sem,
+):
+    me = lax.axis_index("stat")
+    each, par_width = rows.shape[1:]
+    members, stat_width = anomaly_ref.shape
+    barrier = pltpu.get_barrier_semaphore()
+    signal_peers(barrier, me, devices_total)
+    weights = weights_ref[...]
+    for low in range(0, par_width, SLAB):
+        here = slice(low, low + SLAB)
+        change = jnp.dot(weights, spread_ref[:, here], preferred_element_type=jnp.float32)
+        new = params_ref[:, :, here].astype(jnp.float32) + change.reshape(devices_total, each, SLAB)
+        rows[:, :, here] = new.astype(jnp.bfloat16)
+    pl.semaphore_wait(barrier, devices_total - 1)
+
+    def columns(device):
+        return pl.ds(pl.multiple_of(device * par_width, par_width), par_width)
+
+    def copy_to(step, owner):
+        device = lax.rem(me + lax.rem(step * MIX, devices_total), devices_total)
+        if owner is None:
+            owner = lax.rem(
+                me + devices_total - lax.rem(step * MIX, devices_total), devices_total
+            )
+        return pltpu.make_async_remote_copy(
+            src_ref=rows.at[device],
+            dst_ref=updated_ref.at[:, columns(owner)],
+            send_sem=send_sem.at[step],
+            recv_sem=recv_sem.at[step],
+            device_id={"stat": device},
+            device_id_type=MESH,
+        )
+
+    def start(step, carry):
+        copy_to(step, me).start()
+        return carry
+
+    lax.fori_loop(1, devices_total, start, 0)
+    own = pltpu.make_async_copy(rows.at[me], updated_ref.at[:, columns(me)], own_sem)
+    own.start()
+    for slab in range(stat_width // SLAB):
+        here = slice(slab * SLAB, (slab + 1) * SLAB)
+        change = jnp.dot(weights, anomaly_ref[:, here], preferred_element_type=jnp.float32)
+        sigma = jnp.full((1, SLAB), spread_of_group_ref[group_ref[slab]], jnp.float32)
+        raw = closure_ref[:, :, here].astype(jnp.float32).reshape(members, SLAB)
+        predicted_ref[:, here] = (raw + sigma * change).astype(jnp.bfloat16)
+
+    def finish(step, carry):
+        copy_to(step, None).wait_recv()
+        copy_to(step, me).wait_send()
+        return carry
+
+    lax.fori_loop(1, devices_total, finish, 0)
+    own.wait()
+
+
+def update(
+    block_error_group, group_error_spread, weights, closure, anomaly, params, spread
+):
+    devices_total, each, par_width = params.shape
+    vmem = pl.BlockSpec(memory_space=pltpu.VMEM)
+    smem = pl.BlockSpec(memory_space=pltpu.SMEM)
+    return pl.pallas_call(
+        functools.partial(update_kernel, devices_total),
+        out_shape=(
+            jax.ShapeDtypeStruct((each, devices_total * par_width), jnp.bfloat16),
+            jax.ShapeDtypeStruct(anomaly.shape, jnp.bfloat16),
+        ),
+        in_specs=[smem, smem] + [vmem] * 5,
+        out_specs=(vmem, vmem),
+        scratch_shapes=[
+            pltpu.VMEM(params.shape, jnp.bfloat16),
+            pltpu.SemaphoreType.DMA((devices_total,)),
+            pltpu.SemaphoreType.DMA((devices_total,)),
+            pltpu.SemaphoreType.DMA,
+        ],
+        compiler_params=pltpu.CompilerParams(
+            collective_id=1, has_side_effects=True, vmem_limit_bytes=24 * 2**20
+        ),
+        name="update",
+    )(block_error_group, group_error_spread, weights, closure, anomaly, params, spread)
+
+
 def body(
     predicted_moments,
     member_vectors,
@@ -472,8 +636,6 @@
     background_spread,
     member_random_keys,
 ):
-    devices_total = lax.axis_size("stat")
-    stat_width = measured_moments.shape[0]
     total, closure, anomaly, params, spread = exchange(
         predicted_moments,
         member_vectors,
@@ -482,25 +644,12 @@
         group_error_spread,
         background_spread,
         member_random_keys,
-        devices_total,
-    )
-    classes = group_error_spread.shape[0]
-    selector = (block_error_group[:, None] == jnp.arange(classes, dtype=jnp.int32)[None, :]).astype(
-        jnp.float32
-    )
-    slab_sigma = jnp.dot(selector, group_error_spread, precision=lax.Precision.HIGHEST)
-    sigma = jnp.broadcast_to(slab_sigma[:, None], (block_error_group.shape[0], SLAB)).reshape(
-        stat_width
+        lax.axis_size("stat"),
     )
     weights = solve_system(total)
-    updated_rows = (
-        params.astype(jnp.float32) + transposed_product(weights, spread)
-    ).astype(jnp.bfloat16)
-    updated = lax.all_to_all(updated_rows, "stat", split_axis=0, concat_axis=1, tiled=True)
-    predicted = (
-        closure.astype(jnp.float32) + sigma[None, :] * transposed_product(weights, anomaly)
-    ).astype(jnp.bfloat16)
-    return (updated, predicted)
+    return update(
+        block_error_group, group_error_spread, weights, closure, anomaly, params, spread
+    )
 
 
 def solution(mesh):

time: 100 us -> 95.5 us (0.955)
  Pallas kernels: 72.6 us -> 88.6 us
  waiting for transfers between devices: 13.8 us -> 0 us
  starting transfers between devices: 3.49 us -> 0 us
  matrix products: 2.75 us -> 0 us
    pallas_call x0 -> x1, Pallas kernels: none -> 17.6 us  [update(): pl.pallas_call(functools.partial(update_kernel, devices_total), out_shape...]
    all_to_all x1 -> x0, waiting for transfers between devices: 13.8 us -> none  [body(): lax.all_to_all(updated_rows, 'stat', split_axis=0, concat_axis=1, tiled=T...]
    all_to_all x1 -> x0, starting transfers between devices: 3.49 us -> none  [body(): lax.all_to_all(updated_rows, 'stat', split_axis=0, concat_axis=1, tiled=T...]
    dot_general x3 -> x0, matrix products: 2.75 us -> none  [the longest x2 2.56 us: transposed_product(): lax.dot_general(weights, right, (((0,), (0,)), ((), ())), preferred_eleme...]
    pallas_call x1, Pallas kernels: 64.9 us -> 63.2 us  [exchange(): pl.pallas_call(functools.partial(exchange_kernel, stages, devices_total),...]
    unnamed x17 -> x14, local copies, waits for them, and re-layouts: 5.15 us -> 5.39 us
  transfers between devices with their start and end apart: 1 -> 0, of which waited for: 1 -> 0; matrix products, arithmetic and copies ran while one was open for 2% -> 0% of each run, Pallas kernels for 0% -> 0%
where the time goes in v3:
time: 95.5 us; the launch traced here: 95.3 us
  Pallas kernels  88.6 us (93%)
  local copies, waits for them, and re-layouts  5.39 us (6%)
  between operations  1.33 us (1%)
    pallas_call x1, Pallas kernels, exchange(): pl.pallas_call(functools.partial(exchange_kernel, stages, devices_total),...  63.2 us
    pallas_call x1, Pallas kernels, update(): pl.pallas_call(functools.partial(update_kernel, devices_total), out_shape...  17.6 us
    pallas_call x1, Pallas kernels, solve_system(): pl.pallas_call(solve_kernel, out_shape=jax.ShapeDtypeStruct((size, total....  7.8 us
    unnamed x14, local copies, waits for them, and re-layouts  5.39 us

profile of v3, /device:TPU:0, one launch (start us, length us, event | category | flops | bytes accessed | tf_op | source)
XLA Modules:
  0.0 95.3 jit_solution(7183391976781592531)
XLA Ops:
  1.3 0.0 copy-start.5
  1.3 0.0 copy-start.3
  1.3 0.0 copy-start.4
  1.3 0.7 copy-done.5
  2.0 0.0 copy-done.3
  2.0 0.0 copy-done.4
  2.0 0.0 copy-start
  2.0 1.2 %copy-done = bf16[8,65536]{1,0:T(8,128)(2,1)S(1)} copy-done((bf16[8,65536]{1,0:T(8,128)(2,1)S(1)}, bf16[8,65536]{1,0:T(8,128)(2,1)}, u32[]{:S(2)}) %copy-start) | copy-done | bytes 1048600
  3.2 0.0 copy-start.1
  3.2 1.0 %copy-done.1 = bf16[8,32768]{1,0:T(8,128)(2,1)S(1)} copy-done((bf16[8,32768]{1,0:T(8,128)(2,1)S(1)}, bf16[8,32768]{1,0:T(8,128)(2,1)}, u32[]{:S(2)}) %copy-start.1) | copy-done | bytes 524312
  4.2 0.0 copy-start.2
  4.2 0.7 copy-done.2
  4.9 63.2 %exchange.1 = (f32[256,512]{1,0:T(8,128)S(1)}, bf16[32,8,2048]{2,1,0:T(8,128)(2,1)S(1)}, bf16[256,2048]{1,0:T(8,128)(2,1)S(1)}, bf16[32,8,1024]{2,1,0:T(8,128)(2,1)S(1)}, bf16[256,1024]{1,0:T(8,128)(2,1)S(1)}) custom-call(s32[4]{0:T(128)S(1)} %copy-done.3, f32[24]{0:T(128)S(1)} %copy-done.4, f32[1]{0:T(128)S(6)} %copy.11.prior_hbm, s32[1,256]{1,0:T(1,128)S(1)} %bitcast.3, ...), custom_call_target="tpu_custom_call" | custom-call | tf_op jit(solution)/shard_map/exchange/pallas_call | solution.py:404
  68.1 7.8 %solve_system.1.weights_ref = bf16[256,256]{1,0:T(8,128)(2,1)S(1)} custom-call(f32[256,512]{1,0:T(8,128)S(1)} %get-tuple-element.7.s_ref), custom_call_target="tpu_custom_call" | custom-call | tf_op jit(solution)/shard_map/solve_system/pallas_call | solution.py:522
  75.9 17.6 %update.1 = (bf16[8,32768]{1,0:T(8,128)(2,1)S(1)}, bf16[256,2048]{1,0:T(8,128)(2,1)S(1)}) custom-call(s32[4]{0:T(128)S(1)} %copy-done.3, f32[24]{0:T(128)S(1)} %copy-done.4, bf16[256,256]{1,0:T(8,128)(2,1)S(1)} %solve_system.1.weights_ref, bf16[32,8,2048]{2,1,0:T(8,128)(2,1)S(1)} %get-tuple-element.8.closure_ref, ...), custom_call_target="tpu_custom_call" | custom-call | tf_op jit(solution)/shard_map/update/pallas_call | solution.py:609
  93.5 0.8 copy.12
  94.3 1.0 %copy.13 = bf16[256,2048]{1,0:T(8,128)(2,1)} copy(bf16[256,2048]{1,0:T(8,128)(2,1)S(1)} %get-tuple-element.15) | data formatting | bytes 2097152
Async XLA Ops:
  1.3 0.7 copy-start.5
  1.3 0.7 copy-start.3
  1.3 0.7 copy-start.4
  2.0 1.2 %copy-start = (bf16[8,65536]{1,0:T(8,128)(2,1)S(1)}, bf16[8,65536]{1,0:T(8,128)(2,1)}, u32[]{:S(2)}) copy-start(bf16[8,65536]{1,0:T(8,128)(2,1)} %moments_ref.1) | copy-start | bytes 3145732
  3.2 1.0 %copy-start.1 = (bf16[8,32768]{1,0:T(8,128)(2,1)S(1)}, bf16[8,32768]{1,0:T(8,128)(2,1)}, u32[]{:S(2)}) copy-start(bf16[8,32768]{1,0:T(8,128)(2,1)} %vectors_ref.1) | copy-start | bytes 1572868
  4.2 0.7 copy-start.2

commit v4 on v3

--- a/solution.py
+++ b/solution.py
@@ -157,7 +157,7 @@
 
 DRAW_ROWS = 8
 DRAW_LANES = 1024
-MIX = 13
+MIX = 1
 
 
 def exchange_kernel(

time: 95.5 us -> 93.5 us (0.979); the launches traced: 95.3 us -> 91.6 us
  Pallas kernels: 88.6 us -> 84.9 us
    pallas_call x1, Pallas kernels: 17.6 us -> 14.7 us  [update(): pl.pallas_call(functools.partial(update_kernel, devices_total), out_shape...]
where the time goes in v4:
time: 93.5 us; the launch traced here: 91.6 us
  Pallas kernels  84.9 us (91%)
  local copies, waits for them, and re-layouts  5.39 us (6%)
  between operations  1.33 us (1%)
    pallas_call x1, Pallas kernels, exchange(): pl.pallas_call(functools.partial(exchange_kernel, stages, devices_total),...  62.4 us
    pallas_call x1, Pallas kernels, update(): pl.pallas_call(functools.partial(update_kernel, devices_total), out_shape...  14.7 us
    pallas_call x1, Pallas kernels, solve_system(): pl.pallas_call(solve_kernel, out_shape=jax.ShapeDtypeStruct((size, total....  7.79 us
    unnamed x14, local copies, waits for them, and re-layouts  5.39 us

profile of v4, /device:TPU:0, one launch (start us, length us, event | category | flops | bytes accessed | tf_op | source)
XLA Modules:
  0.0 91.6 jit_solution(16272567514811667065)
XLA Ops:
  1.3 0.0 copy-start.5
  1.3 0.0 copy-start.3
  1.3 0.0 copy-start.4
  1.3 0.7 copy-done.5
  2.0 0.0 copy-done.3
  2.0 0.0 copy-done.4
  2.0 0.0 copy-start
  2.0 1.2 %copy-done = bf16[8,65536]{1,0:T(8,128)(2,1)S(1)} copy-done((bf16[8,65536]{1,0:T(8,128)(2,1)S(1)}, bf16[8,65536]{1,0:T(8,128)(2,1)}, u32[]{:S(2)}) %copy-start) | copy-done | bytes 1048600
  3.2 0.0 copy-start.1
  3.2 1.0 %copy-done.1 = bf16[8,32768]{1,0:T(8,128)(2,1)S(1)} copy-done((bf16[8,32768]{1,0:T(8,128)(2,1)S(1)}, bf16[8,32768]{1,0:T(8,128)(2,1)}, u32[]{:S(2)}) %copy-start.1) | copy-done | bytes 524312
  4.2 0.0 copy-start.2
  4.2 0.7 copy-done.2
  4.9 62.4 %exchange.1 = (f32[256,512]{1,0:T(8,128)S(1)}, bf16[32,8,2048]{2,1,0:T(8,128)(2,1)S(1)}, bf16[256,2048]{1,0:T(8,128)(2,1)S(1)}, bf16[32,8,1024]{2,1,0:T(8,128)(2,1)S(1)}, bf16[256,1024]{1,0:T(8,128)(2,1)S(1)}) custom-call(s32[4]{0:T(128)S(1)} %copy-done.3, f32[24]{0:T(128)S(1)} %copy-done.4, f32[1]{0:T(128)S(6)} %copy.11.prior_hbm, s32[1,256]{1,0:T(1,128)S(1)} %bitcast.3, ...), custom_call_target="tpu_custom_call" | custom-call | tf_op jit(solution)/shard_map/exchange/pallas_call | solution.py:404
  67.3 7.8 %solve_system.1.weights_ref = bf16[256,256]{1,0:T(8,128)(2,1)S(1)} custom-call(f32[256,512]{1,0:T(8,128)S(1)} %get-tuple-element.7.s_ref), custom_call_target="tpu_custom_call" | custom-call | tf_op jit(solution)/shard_map/solve_system/pallas_call | solution.py:522
  75.1 14.7 %update.1 = (bf16[8,32768]{1,0:T(8,128)(2,1)S(1)}, bf16[256,2048]{1,0:T(8,128)(2,1)S(1)}) custom-call(s32[4]{0:T(128)S(1)} %copy-done.3, f32[24]{0:T(128)S(1)} %copy-done.4, bf16[256,256]{1,0:T(8,128)(2,1)S(1)} %solve_system.1.weights_ref, bf16[32,8,2048]{2,1,0:T(8,128)(2,1)S(1)} %get-tuple-element.8.closure_ref, ...), custom_call_target="tpu_custom_call" | custom-call | tf_op jit(solution)/shard_map/update/pallas_call | solution.py:609
  89.9 0.8 copy.12
  90.6 1.0 %copy.13 = bf16[256,2048]{1,0:T(8,128)(2,1)} copy(bf16[256,2048]{1,0:T(8,128)(2,1)S(1)} %get-tuple-element.15) | data formatting | bytes 2097152
Async XLA Ops:
  1.3 0.7 copy-start.5
  1.3 0.7 copy-start.3
  1.3 0.7 copy-start.4
  2.0 1.2 %copy-start = (bf16[8,65536]{1,0:T(8,128)(2,1)S(1)}, bf16[8,65536]{1,0:T(8,128)(2,1)}, u32[]{:S(2)}) copy-start(bf16[8,65536]{1,0:T(8,128)(2,1)} %moments_ref.1) | copy-start | bytes 3145732
  3.2 1.0 %copy-start.1 = (bf16[8,32768]{1,0:T(8,128)(2,1)S(1)}, bf16[8,32768]{1,0:T(8,128)(2,1)}, u32[]{:S(2)}) copy-start(bf16[8,32768]{1,0:T(8,128)(2,1)} %vectors_ref.1) | copy-start | bytes 1572868
  4.2 0.7 copy-start.2
